TPU v7x, 32 devices: a whole 2x2x4 slice. The times are simulated.
32 devices in a mesh: seg: 16 (over z, y, x), sub: 2 (over core).
Axes of the slice: x: 2, y: 2, z: 4, core: 2. Of those that a mesh axis runs over, the one named last changes fastest.
Arguments:
- start_field: float32 [3, 221184], P(None, ('seg', 'sub')), may hold values from -6 to 6
- element_loads: float32 [192, 8192], P(None, ('seg', 'sub')), may hold values from -6 to 6
- element_coefs: float32 [2, 8192], P(None, ('seg', 'sub')), may hold values from 0.2 to 5
- element_nodes: int32 [64, 8192], P(None, ('seg', 'sub')), may hold values from 0 to 7295, as said below
- move_list: int32 [3, 8192], P(None, ('seg', 'sub')), may hold values from 0 to 255, as said below
- face_nodes: int32 [2, 6144], P(None, ('seg', 'sub')), may hold values from 0 to 6911, as said below
- stiffness: float32 [2, 192, 192], replicated, as said below
Outputs:
- smoothed: float32 [3, 221184], P(None, ('seg', 'sub'))
- moved_loads: float32 [192, 8192], P(None, ('seg', 'sub'))
- moved_coefs: float32 [2, 8192], P(None, ('seg', 'sub'))
Inputs may be any that keep to these rules, and one draw needn't show every extreme that they name: `move_list`: column e describes the record in slot e of its device before migration: row 0 its destination device p, row 1 its slot there, row 2 its place in the list that its device sends to p. A record that stays keeps its slot and has place 0. Every slot after migration receives exactly one record. A record leaves only for the device just before or after its own, with at most 16 records from one device to each and places below 16, or for a device two or more positions away, with at most 1 records from one device to one such device and places below 1; places are distinct for one source and destination. Both bounds are reached. `element_nodes`: column e lists the nodes of the element in slot e after migration in its device's numbering: values below 6912 are the device's own nodes, 6912 + s is entry s of face_nodes row 1 of the device before, 7104 + s entry s of face_nodes row 0 of the device after. The nodes of one element are distinct, every own node belongs to some element, the first device refers to no device before it and the last to none after it. `face_nodes`: for each device, row 0 lists own nodes that the device before refers to and row 1 those that the device after refers to; the 384 entries of one device are distinct. `stiffness`: both blocks are symmetric with positive diagonals and strictly diagonally dominant rows.
All inputs are finite; a program needn't handle non-finite values.
Results may differ from a plain program's by a relative error of at most 0.0001.
Values sent between devices are 32-bit elements; how exact they have to be, the bound alone decides.
A program may use at most 128 MiB of HBM per device.

v0:
```python
import jax
import jax.numpy as jnp
from jax import lax
from jax.sharding import PartitionSpec as P

NEAR_CAP = 16
DEGREE = 4
SWEEPS = 2


center = 1.125
half_width = 0.875


def shifted(x, axis, by):
    length = lax.axis_size(axis)
    pairs = [(i, i + by) for i in range(length) if 0 <= i + by < length]
    return lax.ppermute(x, axis, pairs)


def local(
    start_field, element_loads, element_coefs, element_nodes, move_list, face_nodes, stiffness
):
    dof_count = element_loads.shape[0]
    slot_count = element_loads.shape[1]
    per_element = element_nodes.shape[0]
    components = dof_count // per_element
    owned_count = start_field.shape[1]
    face_count = face_nodes.shape[1]
    myself = lax.axis_index(("seg", "sub"))
    target_device = move_list[0]
    target_slot = move_list[1]
    list_place = move_list[2]
    staying = target_device == myself
    records = (
        jnp.where(staying[None, :], element_loads, 0.0),
        jnp.where(staying[None, :], element_coefs, 0.0),
    )
    devices = lax.axis_size(("seg", "sub"))
    columns = devices * NEAR_CAP
    where_to = jnp.where(~staying, target_device * NEAR_CAP + list_place, columns)
    packed_loads = (
        jnp.zeros((dof_count, columns), jnp.float32).at[:, where_to].set(element_loads, mode="drop")
    )
    packed_coefs = (
        jnp.zeros((2, columns), jnp.float32).at[:, where_to].set(element_coefs, mode="drop")
    )
    packed_slots = (
        jnp.zeros((1, columns), jnp.int32)
        .at[:, where_to]
        .set((target_slot + 1)[None, :], mode="drop")
    )
    received = (
        lax.all_to_all(packed_loads, ("seg", "sub"), split_axis=1, concat_axis=1, tiled=True),
        lax.all_to_all(packed_coefs, ("seg", "sub"), split_axis=1, concat_axis=1, tiled=True),
        lax.all_to_all(packed_slots, ("seg", "sub"), split_axis=1, concat_axis=1, tiled=True),
    )
    got_slots = received[2][0]
    where_to = jnp.where(got_slots > 0, got_slots - 1, slot_count)
    records = (
        records[0].at[:, where_to].set(received[0], mode="drop"),
        records[1].at[:, where_to].set(received[1], mode="drop"),
    )
    moved_loads, moved_coefs = records
    flat_nodes = element_nodes.reshape(-1)
    back_list = face_nodes[0]
    ahead_list = face_nodes[1]
    blocks = stiffness.reshape(2 * dof_count, dof_count)

    def extend_field(field):
        from_before = shifted(field[:, ahead_list], ("seg", "sub"), 1)
        from_after = shifted(field[:, back_list], ("seg", "sub"), -1)
        return jnp.concatenate([field, from_before, from_after], axis=1)

    def assemble(values):
        channels = values.shape[0] // per_element
        partial_sums = (
            jnp.zeros((channels, owned_count + 2 * face_count), jnp.float32)
            .at[:, flat_nodes]
            .add(values.reshape(channels, -1))
        )
        to_before = partial_sums[:, owned_count : owned_count + face_count]
        to_after = partial_sums[:, owned_count + face_count :]
        from_after = shifted(to_before, ("seg", "sub"), -1)
        from_before = shifted(to_after, ("seg", "sub"), 1)
        return (
            partial_sums[:, :owned_count]
            .at[:, ahead_list]
            .add(from_after)
            .at[:, back_list]
            .add(from_before)
        )

    def operate(field):
        gathered = extend_field(field)[:, flat_nodes].reshape(dof_count, slot_count)
        products = jnp.dot(
            blocks, gathered, precision=lax.Precision.HIGHEST, preferred_element_type=jnp.float32
        )
        return assemble(
            products[:dof_count] * moved_coefs[0] + products[dof_count:] * moved_coefs[1]
        )

    diagonals = jnp.diagonal(stiffness, axis1=1, axis2=2)
    element_diag = diagonals[0][:, None] * moved_coefs[0] + diagonals[1][:, None] * moved_coefs[1]
    totals = assemble(jnp.concatenate([moved_loads, element_diag], axis=0))
    right_side = totals[:components]
    diagonal = totals[components:]
    field = start_field
    scaled_center = center / half_width
    for sweep_index in range(SWEEPS):
        residual = right_side - operate(field)
        update = residual / (center * diagonal)
        ratio = 1.0 / scaled_center
        for degree_step in range(DEGREE):
            field = field + update
            if degree_step + 1 < DEGREE:
                residual = residual - operate(update)
                ratio_next = 1.0 / (2.0 * scaled_center - ratio)
                update = (
                    ratio_next * ratio * update
                    + 2.0 * ratio_next / half_width * residual / diagonal
                )
                ratio = ratio_next
    return (field, moved_loads, moved_coefs)


def solution(mesh):
    return jax.shard_map(
        local,
        mesh=mesh,
        in_specs=(
            P(None, ("seg", "sub")),
            P(None, ("seg", "sub")),
            P(None, ("seg", "sub")),
            P(None, ("seg", "sub")),
            P(None, ("seg", "sub")),
            P(None, ("seg", "sub")),
            P(),
        ),
        out_specs=(P(None, ("seg", "sub")), P(None, ("seg", "sub")), P(None, ("seg", "sub"))),
        check_vma=False,
    )
```

profile of v0, /device:TPU:8, one launch (start us, length us, event | category | flops | bytes accessed | tf_op | source)
XLA Modules:
  0.0 1802.6 jit_solution(378923946374963913)
XLA Ops:
  24.0 9.7 copy.257
  43.5 5.8 all-to-all-start.2
  53.4 56.5 %gather_fusion.3 = f32[16384,3]{1,0:T(8,128)} fusion(f32[3,7296]{0,1:T(8,128)} %pad_maximum_fusion, s32[16384]{0:T(1024)S(1)} %broadcast_clamp_fusion), kind=kCustom, calls=%fused_computation.3 | custom fusion | bytes 458752 | tf_op jit(solution)/shard_map/gather | solution.py:95
  109.9 5.4 copy.269
  115.5 5.8 all-to-all-start.1
  130.9 89.7 %scatter_custom_fusion.8 = f32[3,7296]{0,1:T(8,128)} fusion(s32[16384]{0:T(1024)S(1)} %bitcast.180, f32[16384,3]{1,0:T(8,128)} %copy.271, f32[]{:T(128)} %constant.19.clone.1), kind=kCustom, calls=%fused_computation.72 | custom fusion | flops 49152 | bytes 88064 | tf_op jit(solution)/shard_map/scatter-add | solution.py:80
  228.7 89.7 %scatter_custom_fusion.5 = f32[6,7296]{0,1:T(8,128)} fusion(s32[16384]{0:T(1024)S(1)} %bitcast.181, f32[16384,6]{1,0:T(8,128)} %copy.264, f32[]{:T(128)} %constant.19.clone.1), kind=kCustom, calls=%fused_computation.74 | custom fusion | flops 98304 | bytes 175616 | tf_op jit(solution)/shard_map/scatter-add | solution.py:80
  365.2 7.1 fusion.79
  385.4 5.4 collective-permute-start.7
  400.4 56.5 %gather_fusion.6 = f32[16384,3]{1,0:T(8,128)} fusion(f32[3,7296]{0,1:T(8,128)} %copy.278, s32[16384]{0:T(1024)S(1)} %broadcast_clamp_fusion), kind=kCustom, calls=%fused_computation.6 | custom fusion | bytes 458752 | tf_op jit(solution)/shard_map/gather | solution.py:95
  456.9 5.4 copy.279
  469.1 89.7 %scatter_custom_fusion.11 = f32[3,7296]{0,1:T(8,128)} fusion(s32[16384]{0:T(1024)S(1)} %bitcast.182, f32[16384,3]{1,0:T(8,128)} %copy.281, f32[]{:T(128)} %constant.19.clone.1), kind=kCustom, calls=%fused_computation.70 | custom fusion | flops 49152 | bytes 88064 | tf_op jit(solution)/shard_map/scatter-add | solution.py:80
  603.5 56.5 %gather_fusion.9 = f32[16384,3]{1,0:T(8,128)} fusion(f32[3,7296]{0,1:T(8,128)} %copy.287, s32[16384]{0:T(1024)S(1)} %broadcast_clamp_fusion), kind=kCustom, calls=%fused_computation.9 | custom fusion | bytes 458752 | tf_op jit(solution)/shard_map/gather | solution.py:95
  672.2 89.7 %scatter_custom_fusion.14 = f32[3,7296]{0,1:T(8,128)} fusion(s32[16384]{0:T(1024)S(1)} %bitcast.183, f32[16384,3]{1,0:T(8,128)} %copy.290, f32[]{:T(128)} %constant.19.clone.1), kind=kCustom, calls=%fused_computation.68 | custom fusion | flops 49152 | bytes 88064 | tf_op jit(solution)/shard_map/scatter-add | solution.py:80
  806.7 56.5 %gather_fusion.12 = f32[16384,3]{1,0:T(8,128)} fusion(f32[3,7296]{0,1:T(8,128)} %copy.296, s32[16384]{0:T(1024)S(1)} %broadcast_clamp_fusion), kind=kCustom, calls=%fused_computation.12 | custom fusion | bytes 458752 | tf_op jit(solution)/shard_map/gather | solution.py:95
  875.3 89.7 %scatter_custom_fusion.17 = f32[3,7296]{0,1:T(8,128)} fusion(s32[16384]{0:T(1024)S(1)} %bitcast.184, f32[16384,3]{1,0:T(8,128)} %copy.299, f32[]{:T(128)} %constant.19.clone.1), kind=kCustom, calls=%fused_computation.66 | custom fusion | flops 49152 | bytes 88064 | tf_op jit(solution)/shard_map/scatter-add | solution.py:80
  1009.9 56.5 %gather_fusion.15 = f32[16384,3]{1,0:T(8,128)} fusion(f32[3,7296]{0,1:T(8,128)} %copy.305, s32[16384]{0:T(1024)S(1)} %broadcast_clamp_fusion), kind=kCustom, calls=%fused_computation.15 | custom fusion | bytes 458752 | tf_op jit(solution)/shard_map/gather | solution.py:95
  1078.6 89.7 %scatter_custom_fusion.20 = f32[3,7296]{0,1:T(8,128)} fusion(s32[16384]{0:T(1024)S(1)} %bitcast.185, f32[16384,3]{1,0:T(8,128)} %copy.308, f32[]{:T(128)} %constant.19.clone.1), kind=kCustom, calls=%fused_computation.64 | custom fusion | flops 49152 | bytes 88064 | tf_op jit(solution)/shard_map/scatter-add | solution.py:80
  1213.0 56.5 %gather_fusion.18 = f32[16384,3]{1,0:T(8,128)} fusion(f32[3,7296]{0,1:T(8,128)} %copy.314, s32[16384]{0:T(1024)S(1)} %broadcast_clamp_fusion), kind=kCustom, calls=%fused_computation.18 | custom fusion | bytes 458752 | tf_op jit(solution)/shard_map/gather | solution.py:95
  1281.6 89.7 %scatter_custom_fusion.23 = f32[3,7296]{0,1:T(8,128)} fusion(s32[16384]{0:T(1024)S(1)} %bitcast.186, f32[16384,3]{1,0:T(8,128)} %copy.317, f32[]{:T(128)} %constant.19.clone.1), kind=kCustom, calls=%fused_computation.62 | custom fusion | flops 49152 | bytes 88064 | tf_op jit(solution)/shard_map/scatter-add | solution.py:80
  1416.1 56.5 %gather_fusion.21 = f32[16384,3]{1,0:T(8,128)} fusion(f32[3,7296]{0,1:T(8,128)} %copy.323, s32[16384]{0:T(1024)S(1)} %broadcast_clamp_fusion), kind=kCustom, calls=%fused_computation.21 | custom fusion | bytes 458752 | tf_op jit(solution)/shard_map/gather | solution.py:95
  1484.8 89.7 %scatter_custom_fusion.26 = f32[3,7296]{0,1:T(8,128)} fusion(s32[16384]{0:T(1024)S(1)} %bitcast.187, f32[16384,3]{1,0:T(8,128)} %copy.326, f32[]{:T(128)} %constant.19.clone.1), kind=kCustom, calls=%fused_computation.60 | custom fusion | flops 49152 | bytes 88064 | tf_op jit(solution)/shard_map/scatter-add | solution.py:80
  1619.2 56.5 %gather_fusion.24 = f32[16384,3]{1,0:T(8,128)} fusion(f32[3,7296]{0,1:T(8,128)} %copy.332, s32[16384]{0:T(1024)S(1)} %broadcast_clamp_fusion), kind=kCustom, calls=%fused_computation.24 | custom fusion | bytes 458752 | tf_op jit(solution)/shard_map/gather | solution.py:95
  1687.9 89.7 %scatter_custom_fusion.29 = f32[3,7296]{0,1:T(8,128)} fusion(s32[16384]{0:T(1024)S(1)} %bitcast.188, f32[16384,3]{1,0:T(8,128)} %copy.335, f32[]{:T(128)} %constant.19.clone.1), kind=kCustom, calls=%fused_computation.58 | custom fusion | flops 49152 | bytes 88064 | tf_op jit(solution)/shard_map/scatter-add | solution.py:80
  (282 shorter events, 496.5 us)
Async XLA Ops:
  7.3 42.0 %collective-permute-start.2 = (f32[3,192]{0,1:T(8,128)S(1)}, f32[3,192]{0,1:T(8,128)S(1)}, u32[]{:S(2)}, u32[]{:S(2)}) collective-permute-start(f32[3,192]{0,1:T(8,128)S(1)} %bitcast.233), channel_id=1, source_target_pairs={{0,1},{1,2},{2,3},{3,4},{4,5},{5,6},{6,7},{7,8},{8,9},{9,10},{10,1... | collective-permute-start | bytes 6920 | tf_op jit(solution)/shard_map/ppermute | solution.py:18
  11.9 37.4 %collective-permute-start.3 = (f32[3,192]{0,1:T(8,128)S(1)}, f32[3,192]{0,1:T(8,128)S(1)}, u32[]{:S(2)}, u32[]{:S(2)}) collective-permute-start(f32[3,192]{0,1:T(8,128)S(1)} %bitcast.234), channel_id=1, source_target_pairs={{1,0},{2,1},{3,2},{4,3},{5,4},{6,5},{7,6},{8,7},{9,8},{10,9},{11,1... | collective-permute-start | bytes 6920 | tf_op jit(solution)/shard_map/ppermute | solution.py:18
  19.5 23.9 %all-to-all-start = ((s32[1,32,16]{2,0,1:T(1,128)}), s32[1,32,16]{2,0,1:T(1,128)S(1)}, u32[]{:S(2)}, u32[]{:S(2)}) async-start(s32[1,32,16]{2,0,1:T(1,128)} %bitcast.4), calls=%async_computation | async-start | bytes 32768 | tf_op jit(solution)/shard_map/all_to_all | solution.py:56
  43.5 72.1 %all-to-all-start.2 = ((f32[2,32,16]{2,0,1:T(2,128)}), f32[2,32,16]{2,0,1:T(2,128)S(1)}, u32[]{:S(2)}, u32[]{:S(2)}) async-start(f32[2,32,16]{2,0,1:T(2,128)} %copy.259), calls=%async_computation.2 | async-start | bytes 65536 | tf_op jit(solution)/shard_map/all_to_all | solution.py:55
  115.5 105.0 %all-to-all-start.1 = ((f32[192,32,16]{0,2,1:T(8,128)}), f32[192,32,16]{0,2,1:T(8,128)S(1)}, u32[]{:S(2)}, u32[]{:S(2)}) async-start(f32[192,32,16]{0,2,1:T(8,128)} %bitcast.7), calls=%async_computation.1 | async-start | bytes 1048576 | tf_op jit(solution)/shard_map/all_to_all | solution.py:54
  319.3 35.3 %collective-permute-start = (f32[6,192]{0,1:T(8,128)S(1)}, f32[6,192]{0,1:T(8,128)S(1)}, u32[]{:S(2)}, u32[]{:S(2)}) collective-permute-start(f32[6,192]{0,1:T(8,128)S(1)} %get-tuple-element.54), channel_id=1, source_target_pairs={{1,0},{2,1},{3,2},{4,3},{5,4},{6,5},{7,6},{8,7},{9,8},{10,9},{11,1... | collective-permute-start | bytes 13832 | tf_op jit(solution)/shard_map/ppermute | solution.py:18
  323.3 36.6 %collective-permute-start.1 = (f32[6,192]{0,1:T(8,128)S(1)}, f32[6,192]{0,1:T(8,128)S(1)}, u32[]{:S(2)}, u32[]{:S(2)}) collective-permute-start(f32[6,192]{0,1:T(8,128)S(1)} %get-tuple-element.53), channel_id=1, source_target_pairs={{0,1},{1,2},{2,3},{3,4},{4,5},{5,6},{6,7},{7,8},{8,9},{9,10},{10,1... | collective-permute-start | bytes 13832 | tf_op jit(solution)/shard_map/ppermute | solution.py:18
  326.2 11.4 collective-permute-start.4
  331.7 11.1 collective-permute-start.5
  385.4 7.5 collective-permute-start.7
  559.7 8.3 collective-permute-start.8
  561.7 11.6 collective-permute-start.9
  762.9 8.3 collective-permute-start.12
  764.8 11.6 collective-permute-start.13
  966.0 8.3 collective-permute-start.16
  967.9 11.6 collective-permute-start.17
  1169.2 8.3 collective-permute-start.20
  1171.1 11.6 collective-permute-start.21
  1372.3 8.3 collective-permute-start.24
  1374.2 11.6 collective-permute-start.25
  1575.4 8.3 collective-permute-start.28
  1577.3 11.6 collective-permute-start.29
  1778.5 9.8 collective-permute-start.32
  1780.4 13.1 collective-permute-start.33
  (19 other events, 181.1 us)
where the time goes:
time: 1810 us; the launch traced here: 1800 us
  other arithmetic  910 us (50%)
  local copies, waits for them, and re-layouts  733 us (40%)
  starting transfers between devices  117 us (6%)
  waiting for transfers between devices  32 us (2%)
    scatter-add x9, other arithmetic, assemble(): partial_sums = jnp.zeros((channels, owned_count + 2 * face_count), jnp.fl...  807 us
    gather x16, local copies, waits for them, and re-layouts, operate(): gathered = extend_field(field)[:, flat_nodes].reshape(dof_count, slot_count)  495 us
    ppermute x34, starting transfers between devices, shifted(): return lax.ppermute(x, axis, pairs)  101 us
    scatter-add x18, other arithmetic, assemble(): return partial_sums[:, :owned_count].at[:, ahead_list].add(from_after).at...  94.1 us
    reshape x18, local copies, waits for them, and re-layouts, assemble(): values.reshape(channels, -1)  46.9 us
  transfers between devices with their start and end apart: 37, of which 7 were waited for; matrix products, arithmetic and copies ran while one was open for 16% of the time, Pallas kernels for 0%

commit v1 on v0

v1 whole, which is shorter than its diff:
```python
import functools

import jax
import jax.numpy as jnp
from jax import lax
from jax.experimental import pallas as pl
from jax.experimental.pallas import tpu as pltpu
from jax.sharding import PartitionSpec as P

NEAR_CAP = 16
DEGREE = 4
SWEEPS = 2
LOW = 32
GROUP = 8
LANES = 128

center = 1.125
half_width = 0.875

f32 = jnp.float32
bf16 = jnp.bfloat16
i32 = jnp.int32
HIGHEST = lax.Precision.HIGHEST


def chebyshev_weights():
    weights = []
    scaled_center = center / half_width
    for sweep_index in range(SWEEPS):
        if sweep_index:
            weights.append((0.0, 1.0 / center))
        ratio = 1.0 / scaled_center
        for _ in range(DEGREE - 1):
            ratio_next = 1.0 / (2.0 * scaled_center - ratio)
            weights.append((ratio_next * ratio, 2.0 * ratio_next / half_width))
            ratio = ratio_next
    return weights


def split(x):
    high = x.astype(bf16)
    return high, (x - high.astype(f32)).astype(bf16)


def dot(a, b):
    return jnp.dot(a, b, preferred_element_type=f32)


def dot_nt(a, b, precision=None):
    return lax.dot_general(
        a, b, (((1,), (1,)), ((), ())), precision=precision, preferred_element_type=f32
    )


def pick_low(found, low_row, components):
    mask = lax.broadcasted_iota(i32, (LOW, low_row.shape[1]), 0) == low_row
    half = components * LOW
    both = found[:half] + found[half:]
    return [
        jnp.sum(jnp.where(mask, both[c * LOW : (c + 1) * LOW], 0.0), axis=0, keepdims=True)
        for c in range(components)
    ]


def spread_low(rows, low_row):
    mask = lax.broadcasted_iota(i32, (LOW, low_row.shape[1]), 0) == low_row
    tall = []
    for part in range(2):
        for row in rows:
            high = row.astype(bf16).astype(f32)
            piece = high if part == 0 else row - high
            tall.append(jnp.where(mask, piece, 0.0).astype(bf16))
    return jnp.concatenate(tall, axis=0)


def one_hot_rows(row, count):
    hit = lax.broadcasted_iota(i32, (count, row.shape[1]), 0) == row
    return jnp.where(hit, 1.0, 0.0).astype(bf16)


def kernel(
    devices, subs, owned, face,
    start_ref, loads_ref, coefs_ref, nodes_ref, moves_ref, face_smem, face_ref, stiff_ref,
    out_ref, moved_loads_ref, moved_coefs_ref,
    onehot, onehot_t, column_t, high_ref, low_ref, stiff_high, stiff_low, x_ref, y_ref,
    update_ref, residual_ref, inverse_ref, delta_ref, total_ref,
    far_out, far_in, near_out, near_in, records, edge_out, edge_in,
    far_send, far_recv, near_send, near_recv, edge_send, edge_recv,
):
    per_element, slots = nodes_ref.shape
    dofs = loads_ref.shape[0]
    components = dofs // per_element
    height = components * LOW
    columns = owned // LOW
    width = face // LOW
    table = onehot.shape[1]
    groups = per_element // GROUP
    me = lax.axis_index("seg") * subs + lax.axis_index("sub")
    has_prev = me > 0
    has_next = me < devices - 1

    def coords(p):
        return {"seg": lax.div(p, subs), "sub": lax.rem(p, subs)}

    before = coords(jnp.maximum(me - 1, 0))
    after = coords(jnp.minimum(me + 1, devices - 1))

    far_in[me] = jnp.zeros((1, slots), f32)
    near_in[...] = jnp.zeros_like(near_in)
    barrier = pltpu.get_barrier_semaphore()

    def greet(d, _):
        pl.semaphore_signal(
            barrier, inc=1, device_id=coords(lax.rem(me + d, devices)),
            device_id_type=pl.DeviceIdType.MESH,
        )
        return 0

    lax.fori_loop(1, devices, greet, 0)

    def edge_copy(way, t):
        return pltpu.make_async_remote_copy(
            src_ref=edge_out.at[t], dst_ref=edge_in.at[way, t],
            send_sem=edge_send.at[way, t], recv_sem=edge_recv.at[way, t],
            device_id=after if way == 0 else before, device_id_type=pl.DeviceIdType.MESH,
        )

    def near_copy(way):
        return pltpu.make_async_remote_copy(
            src_ref=near_out.at[way], dst_ref=near_in.at[way],
            send_sem=near_send.at[way], recv_sem=near_recv.at[way],
            device_id=after if way == 0 else before, device_id_type=pl.DeviceIdType.MESH,
        )

    def both_ways(copies):
        @pl.when(has_next)
        def _():
            copies[0].start()

        @pl.when(has_prev)
        def _():
            copies[1].start()

    def finish(copies):
        @pl.when(has_prev)
        def _():
            copies[0].wait_recv()
            copies[1].wait_send()

        @pl.when(has_next)
        def _():
            copies[1].wait_recv()
            copies[0].wait_send()

    def send_edge(part, t):
        edge_out[t] = part[:, table - LANES :]
        both_ways([edge_copy(0, t), edge_copy(1, t)])

    lane = lax.broadcasted_iota(i32, (height, LANES), 1) - (columns - (table - LANES))

    def receive_edge(part, t):
        finish([edge_copy(0, t), edge_copy(1, t)])
        from_prev = pltpu.roll(edge_in[0, t], 2 * width, 1)
        from_next = pltpu.roll(edge_in[1, t], LANES - 2 * width, 1)
        take_prev = (lane >= 2 * width) & (lane < 4 * width) & has_prev
        take_next = (lane >= 0) & (lane < 2 * width) & has_next
        tail = part[:, table - LANES :]
        tail = tail + jnp.where(take_prev, from_prev, jnp.where(take_next, from_next, 0.0))
        return jnp.concatenate([part[:, : table - LANES], tail], axis=1)

    face_row = face_ref[...]
    face_low = ((face_row.astype(f32) + 0.5) * (1.0 / columns)).astype(i32)
    face_old = one_hot_rows(face_row - face_low * columns, table)
    place = lax.broadcasted_iota(i32, face_row.shape, 1)
    face_new_low = place & (LOW - 1)
    face_new = one_hot_rows(lax.div(place, LOW) + columns + width, table)

    start = jnp.concatenate(
        [start_ref[...], jnp.zeros((height, table - columns), f32)], axis=1
    )
    face_values = pick_low(dot(jnp.concatenate(split(start), 0), face_old), face_low, components)
    lifted = dot_nt(spread_low(face_values, face_new_low), face_new)
    field = start + lifted[:height] + lifted[height:]

    dest = moves_ref[0:1, :]
    new_slot = moves_ref[1:2, :]
    spot = moves_ref[2:3, :]
    staying = dest == me
    row_of = jnp.where(
        dest == me + 1, devices + spot,
        jnp.where(dest == me - 1, devices + NEAR_CAP + spot, dest),
    )
    row_of = jnp.where(staying, -1, row_of)
    record = jnp.concatenate(
        [
            loads_ref[...], coefs_ref[...], (new_slot + 1).astype(f32),
            jnp.zeros((slots - dofs - 3, slots), f32),
        ],
        axis=0,
    )
    rows = devices + 2 * NEAR_CAP
    chosen = lax.broadcasted_iota(i32, (rows, slots), 0) == row_of
    packed = dot_nt(jnp.where(chosen, 1.0, 0.0), record, HIGHEST)
    for p in range(devices):
        far_out[p] = packed[p : p + 1]
    near_out[0] = packed[devices : devices + NEAR_CAP]
    near_out[1] = packed[devices + NEAR_CAP :]

    def far_copy(p, row):
        return pltpu.make_async_remote_copy(
            src_ref=far_out.at[p], dst_ref=far_in.at[row],
            send_sem=far_send.at[p], recv_sem=far_recv.at[row],
            device_id=coords(p), device_id_type=pl.DeviceIdType.MESH,
        )

    pl.semaphore_wait(barrier, devices - 1)
    send_edge(field, 0)
    both_ways([near_copy(0), near_copy(1)])

    def far_start(d, _):
        far_copy(lax.rem(me + d, devices), me).start()
        return 0

    lax.fori_loop(1, devices, far_start, 0)

    nodes = nodes_ref[...]
    extra = jnp.where(
        nodes < owned, -1, jnp.where(nodes < owned + face, nodes - owned + 3 * face, nodes - owned - face)
    )

    def relabel(s, extra):
        extra = jnp.where(nodes == face_smem[1, s], face + s, extra)
        return jnp.where(nodes == face_smem[0, s], 2 * face + s, extra)

    extra = lax.fori_loop(0, face, relabel, extra, unroll=4)
    own_low = ((nodes.astype(f32) + 0.5) * (1.0 / columns)).astype(i32)
    low = jnp.where(extra >= 0, extra & (LOW - 1), own_low)
    high = jnp.where(extra >= 0, columns + lax.div(extra, LOW), nodes - own_low * columns)
    high_ref[...] = high
    low_ref[...] = low
    high_t = jnp.transpose(high.astype(f32)).astype(i32)
    for g in range(groups):
        column_t[g] = high_t[:, g * GROUP : (g + 1) * GROUP]

    def build(g, _):
        own = column_t[g]
        rows8 = high_ref[pl.ds(pl.multiple_of(g * GROUP, GROUP), GROUP), :]
        for j in range(GROUP):
            n = g * GROUP + j
            onehot[n] = one_hot_rows(rows8[j : j + 1], table)
            hit = lax.broadcasted_iota(i32, (slots, table), 1) == own[:, j : j + 1]
            onehot_t[pl.ds(pl.multiple_of(n * slots, slots), slots), :] = jnp.where(
                hit, 1.0, 0.0
            ).astype(bf16)
        return 0

    lax.fori_loop(0, groups, build, 0)

    stiff = stiff_ref[...]
    stiff_high[...] = stiff.astype(bf16)
    stiff_low[...] = (stiff - stiff_high[...].astype(f32)).astype(bf16)

    def gather(values):
        both = jnp.concatenate(split(values), axis=0)

        def step(g, _):
            low8 = low_ref[pl.ds(pl.multiple_of(g * GROUP, GROUP), GROUP), :]
            found = [[] for _ in range(components)]
            for j in range(GROUP):
                rows = pick_low(dot(both, onehot[g * GROUP + j]), low8[j : j + 1], components)
                for c in range(components):
                    found[c].append(rows[c])
            for c in range(components):
                at = pl.multiple_of(c * per_element + g * GROUP, GROUP)
                x_ref[pl.ds(at, GROUP), :] = jnp.concatenate(found[c], axis=0)
            return 0

        lax.fori_loop(0, groups, step, 0)

    def scatter(values):
        y_ref[...] = values
        total_ref[...] = jnp.zeros_like(total_ref)

        def step(g, _):
            low8 = low_ref[pl.ds(pl.multiple_of(g * GROUP, GROUP), GROUP), :]
            parts = [
                y_ref[pl.ds(pl.multiple_of(c * per_element + g * GROUP, GROUP), GROUP), :]
                for c in range(components)
            ]
            wide = jnp.concatenate(
                [
                    spread_low([part[j : j + 1] for part in parts], low8[j : j + 1])
                    for j in range(GROUP)
                ],
                axis=1,
            )
            at = pl.multiple_of(g * GROUP * slots, GROUP * slots)
            total_ref[...] += dot(wide, onehot_t[pl.ds(at, GROUP * slots), :])
            return 0

        lax.fori_loop(0, groups, step, 0)
        return total_ref[:height] + total_ref[height:]

    def products():
        x_high, x_low = split(x_ref[...])
        return dot(stiff_high[...], x_high) + (
            dot(stiff_low[...], x_high) + dot(stiff_high[...], x_low)
        )

    field = receive_edge(field, 0)
    gather(field)
    both = products()

    finish([near_copy(0), near_copy(1)])

    def far_finish(d, _):
        p = lax.rem(me + d, devices)
        far_copy(p, p).wait_recv()
        far_copy(p, p).wait_send()
        return 0

    lax.fori_loop(1, devices, far_finish, 0)
    records[...] = jnp.zeros_like(records)
    for p in range(devices):
        records[p : p + 1, :] = far_in[p]
    records[devices : devices + NEAR_CAP, :] = near_in[0]
    records[devices + NEAR_CAP : devices + 2 * NEAR_CAP, :] = near_in[1]
    got = records[...]
    slot_of = got[:, dofs + 2 : dofs + 3]
    aim = lax.broadcasted_iota(i32, (got.shape[0], slots), 1).astype(f32) + 1.0
    landing = jnp.where(aim == slot_of, 1.0, 0.0)
    arrived = jnp.dot(
        jnp.transpose(got), landing, precision=HIGHEST, preferred_element_type=f32
    )
    moved = jnp.where(staying, record, 0.0) + arrived
    loads = moved[:dofs]
    coefs = moved[dofs : dofs + 2]
    moved_loads_ref[...] = loads
    moved_coefs_ref[...] = coefs
    first, second = coefs[0:1], coefs[1:2]

    def element_values(both):
        return both[:dofs] * first + both[dofs:] * second

    on_diagonal = lax.broadcasted_iota(i32, (dofs, dofs), 0) == lax.broadcasted_iota(
        i32, (dofs, dofs), 1
    )
    diagonals = [
        jnp.sum(jnp.where(on_diagonal, stiff[k * dofs : (k + 1) * dofs], 0.0), axis=1, keepdims=True)
        for k in range(2)
    ]
    part = scatter(loads - element_values(both))
    send_edge(part, 1)
    diagonal = scatter(diagonals[0] * first + diagonals[1] * second)
    send_edge(diagonal, 2)
    residual = receive_edge(part, 1)
    diagonal = receive_edge(diagonal, 2)
    inverse = jnp.where(diagonal > 0.0, 1.0 / diagonal, 0.0)
    inverse_ref[...] = inverse
    residual_ref[...] = residual
    update_ref[...] = residual * inverse * (1.0 / center)
    delta_ref[...] = jnp.zeros_like(delta_ref)
    weights = chebyshev_weights()

    def sweep_step(i, _):
        update = update_ref[...]
        delta_ref[...] += update
        gather(update)
        part = scatter(element_values(products()))
        send_edge(part, 3 + i)
        residual = residual_ref[...] - receive_edge(part, 3 + i)
        residual_ref[...] = residual
        old, new = jnp.float32(0.0), jnp.float32(0.0)
        for k, (a, b) in enumerate(weights):
            old = jnp.where(i == k, a, old)
            new = jnp.where(i == k, b, new)
        update_ref[...] = old * update + new * (residual * inverse_ref[...])
        return 0

    lax.fori_loop(0, len(weights), sweep_step, 0)

    delta = delta_ref[...] + update_ref[...]
    face_values = pick_low(
        dot(jnp.concatenate(split(delta), 0), face_new), face_new_low, components
    )
    lowered = dot_nt(spread_low(face_values, face_low), face_old)
    result = start + delta + lowered[:height] + lowered[height:]
    out_ref[...] = result[:, :columns]


def local(
    devices, subs,
    start_field, element_loads, element_coefs, element_nodes, move_list, face_nodes, stiffness,
):
    dofs, slots = element_loads.shape
    per_element = element_nodes.shape[0]
    components = dofs // per_element
    owned = start_field.shape[1]
    face = face_nodes.shape[1]
    height = components * LOW
    columns = owned // LOW
    table = -(-(columns + 4 * (face // LOW)) // LANES) * LANES
    groups = per_element // GROUP
    rows = -(-(devices + 2 * NEAR_CAP) // LANES) * LANES
    edges = 2 + SWEEPS * DEGREE
    vmem = pl.BlockSpec(memory_space=pltpu.VMEM)
    smem = pl.BlockSpec(memory_space=pltpu.SMEM)
    wide = (height, table)
    smoothed, moved_loads, moved_coefs = pl.pallas_call(
        functools.partial(kernel, devices, subs, owned, face),
        out_shape=(
            jax.ShapeDtypeStruct((height, columns), f32),
            jax.ShapeDtypeStruct((dofs, slots), f32),
            jax.ShapeDtypeStruct((2, slots), f32),
        ),
        in_specs=[vmem] * 5 + [smem, vmem, vmem],
        out_specs=(vmem, vmem, vmem),
        scratch_shapes=[
            pltpu.VMEM((per_element, table, slots), bf16),
            pltpu.VMEM((per_element * slots, table), bf16),
            pltpu.VMEM((groups, slots, GROUP), i32),
            pltpu.VMEM((per_element, slots), i32),
            pltpu.VMEM((per_element, slots), i32),
            pltpu.VMEM((2 * dofs, dofs), bf16),
            pltpu.VMEM((2 * dofs, dofs), bf16),
            pltpu.VMEM((dofs, slots), f32),
            pltpu.VMEM((dofs, slots), f32),
            pltpu.VMEM(wide, f32),
            pltpu.VMEM(wide, f32),
            pltpu.VMEM(wide, f32),
            pltpu.VMEM(wide, f32),
            pltpu.VMEM((2 * height, table), f32),
            pltpu.VMEM((devices, 1, slots), f32),
            pltpu.VMEM((devices, 1, slots), f32),
            pltpu.VMEM((2, NEAR_CAP, slots), f32),
            pltpu.VMEM((2, NEAR_CAP, slots), f32),
            pltpu.VMEM((rows, slots), f32),
            pltpu.VMEM((edges, height, LANES), f32),
            pltpu.VMEM((2, edges, height, LANES), f32),
            pltpu.SemaphoreType.DMA((devices,)),
            pltpu.SemaphoreType.DMA((devices,)),
            pltpu.SemaphoreType.DMA((2,)),
            pltpu.SemaphoreType.DMA((2,)),
            pltpu.SemaphoreType.DMA((2, edges)),
            pltpu.SemaphoreType.DMA((2, edges)),
        ],
        compiler_params=pltpu.CompilerParams(
            collective_id=0, has_side_effects=True, vmem_limit_bytes=48 * 1024 * 1024
        ),
        name="migrate_and_smooth",
    )(
        start_field.reshape(height, columns),
        element_loads,
        element_coefs,
        element_nodes,
        move_list,
        face_nodes,
        jnp.concatenate([face_nodes[1], face_nodes[0]])[None, :],
        stiffness.reshape(2 * dofs, dofs),
    )
    return smoothed.reshape(components, owned), moved_loads, moved_coefs


def solution(mesh):
    devices = mesh.shape["seg"] * mesh.shape["sub"]
    return jax.shard_map(
        functools.partial(local, devices, mesh.shape["sub"]),
        mesh=mesh,
        in_specs=(
            P(None, ("seg", "sub")),
            P(None, ("seg", "sub")),
            P(None, ("seg", "sub")),
            P(None, ("seg", "sub")),
            P(None, ("seg", "sub")),
            P(None, ("seg", "sub")),
            P(),
        ),
        out_specs=(P(None, ("seg", "sub")), P(None, ("seg", "sub")), P(None, ("seg", "sub"))),
        check_vma=False,
    )
```

time: 1810 us -> 107 us (0.06)
  other arithmetic: 910 us -> 0.08 us
  local copies, waits for them, and re-layouts: 733 us -> 5.75 us
  starting transfers between devices: 117 us -> 0 us
  Pallas kernels: 0 us -> 100 us
  waiting for transfers between devices: 32 us -> 0 us
    scatter-add x27 -> x0, other arithmetic: 901 us -> none  [the longest x9 807 us: assemble(): partial_sums = jnp.zeros((channels, owned_count + 2 * face_count), jnp.fl...]
    gather x47 -> x0, local copies, waits for them, and re-layouts: 544 us -> none  [the longest x16 495 us: operate(): gathered = extend_field(field)[:, flat_nodes].reshape(dof_count, slot_count)]
    ppermute x34 -> x0, starting transfers between devices: 101 us -> none  [shifted(): return lax.ppermute(x, axis, pairs)]
    pallas_call x0 -> x1, Pallas kernels: none -> 100 us  [local(): pl.pallas_call(functools.partial(kernel, devices, subs, owned, face), out...]
    slice x21 -> x1, local copies, waits for them, and re-layouts: 52 us -> 0.76 us  [local(): face_nodes[1]]
    reshape x26 -> x2, local copies, waits for them, and re-layouts: 48.1 us -> 1.89 us  [the longest x1 1.09 us: local(): start_field.reshape(height, columns)]
    ppermute x34 -> x0, waiting for transfers between devices: 32 us -> none  [shifted(): return lax.ppermute(x, axis, pairs)]
    scatter-add x8 -> x0, local copies, waits for them, and re-layouts: 20.5 us -> none  [assemble(): return partial_sums[:, :owned_count].at[:, ahead_list].add(from_after).at...]
  transfers between devices with their start and end apart: 37 -> 0, of which waited for: 7 -> 0; matrix products, arithmetic and copies ran while one was open for 16% -> 0% of each run, Pallas kernels for 0% -> 0%
where the time goes in v1:
time: 107 us
  Pallas kernels  100 us (93%)
  local copies, waits for them, and re-layouts  5.75 us (5%)
    pallas_call x1, Pallas kernels, local(): pl.pallas_call(functools.partial(kernel, devices, subs, owned, face), out...  100 us
    unnamed x14, local copies, waits for them, and re-layouts  3.1 us

profile of v1, /device:TPU:8, one launch (start us, length us, event | category | flops | bytes accessed | tf_op | source)
XLA Modules:
  0.0 106.7 jit_solution(6052053444504208020)
XLA Ops:
  0.6 0.0 copy-start.1
  0.6 0.8 fusion
  1.4 0.1 pad_add_fusion
  1.5 0.0 copy-start.3
  1.5 0.0 copy-start.4
  1.5 0.0 copy-start.5
  1.5 1.1 %reshape.15.start_ref = f32[96,216]{1,0:T(8,128)S(1)} reshape(f32[3,6912]{1,0:T(4,128)} %param.7) | data formatting | bytes 165888 | tf_op jit(solution)/shard_map/reshape | solution.py:452
  2.6 0.0 copy-done.1
  2.6 0.0 copy-done.3
  2.6 0.0 copy-done.4
  2.6 0.0 copy-done.5
  2.6 0.0 copy-start
  2.6 1.0 copy-done
  3.6 0.0 copy-start.2
  3.6 0.8 copy-done.2
  4.5 100.2 %migrate_and_smooth.1 = (f32[96,216]{1,0:T(8,128)S(1)}, f32[192,256]{1,0:T(8,128)S(1)}, f32[2,256]{1,0:T(2,128)S(1)}) custom-call(f32[96,216]{1,0:T(8,128)S(1)} %reshape.15.start_ref, f32[192,256]{1,0:T(8,128)S(1)} %copy-done.1, f32[2,256]{1,0:T(2,128)S(1)} %copy-done.5, s32[64,256]{1,0:T(8,128)S(1)} %copy-done.2, s32[3,256]{1,0:T(4,128)S(1)} %copy-done.4, ...), custom_call_target="tpu_custom_call" | custom-call | tf_op jit(solution)/shard_map/migrate_and_smooth/pallas_call | solution.py:409
  104.6 0.8 reshape.17
  105.4 0.7 copy.12
  106.1 0.6 copy.13
  (1 shorter events, 0.0 us)
Async XLA Ops:
  0.6 2.0 %copy-start.1 = (f32[192,256]{1,0:T(8,128)S(1)}, f32[192,256]{1,0:T(8,128)}, u32[]{:S(2)}) copy-start(f32[192,256]{1,0:T(8,128)} %loads_ref.1) | copy-start | bytes 589828
  1.5 1.1 %copy-start.3 = (s32[2,192]{1,0:T(2,128)S(1)}, s32[2,192]{1,0:T(2,128)}, u32[]{:S(2)}) copy-start(s32[2,192]{1,0:T(2,128)} %face_smem.1) | copy-start | bytes 4612
  1.5 1.1 %copy-start.4 = (s32[3,256]{1,0:T(4,128)S(1)}, s32[3,256]{1,0:T(4,128)}, u32[]{:S(2)}) copy-start(s32[3,256]{1,0:T(4,128)} %moves_ref.1) | copy-start | bytes 9220
  1.5 1.1 %copy-start.5 = (f32[2,256]{1,0:T(2,128)S(1)}, f32[2,256]{1,0:T(2,128)}, u32[]{:S(2)}) copy-start(f32[2,256]{1,0:T(2,128)} %coefs_ref.1) | copy-start | bytes 6148
  2.6 1.0 copy-start
  3.6 0.8 copy-start.2

commit v2 on v1

--- a/solution.py
+++ b/solution.py
@@ -10,9 +10,11 @@
 NEAR_CAP = 16
 DEGREE = 4
 SWEEPS = 2
-LOW = 32
+COLUMNS = 256
+TILE = 8
 GROUP = 8
 LANES = 128
+UNROLL = 4
 
 center = 1.125
 half_width = 0.875
@@ -53,17 +55,18 @@
 
 
 def pick_low(found, low_row, components):
-    mask = lax.broadcasted_iota(i32, (LOW, low_row.shape[1]), 0) == low_row
-    half = components * LOW
+    half = found.shape[0] // 2
+    depth = half // components
+    mask = lax.broadcasted_iota(i32, (depth, low_row.shape[1]), 0) == low_row
     both = found[:half] + found[half:]
     return [
-        jnp.sum(jnp.where(mask, both[c * LOW : (c + 1) * LOW], 0.0), axis=0, keepdims=True)
+        jnp.sum(jnp.where(mask, both[c * depth : (c + 1) * depth], 0.0), axis=0, keepdims=True)
         for c in range(components)
     ]
 
 
-def spread_low(rows, low_row):
-    mask = lax.broadcasted_iota(i32, (LOW, low_row.shape[1]), 0) == low_row
+def spread_low(rows, low_row, depth):
+    mask = lax.broadcasted_iota(i32, (depth, low_row.shape[1]), 0) == low_row
     tall = []
     for part in range(2):
         for row in rows:
@@ -79,26 +82,38 @@
 
 
 def kernel(
-    devices, subs, owned, face,
-    start_ref, loads_ref, coefs_ref, nodes_ref, moves_ref, face_smem, face_ref, stiff_ref,
+    devices, subs,
+    start_hbm, loads_hbm, coefs_ref, nodes_hbm, moves_ref, face_smem, face_ref, stiff_hbm,
     out_ref, moved_loads_ref, moved_coefs_ref,
-    onehot, onehot_t, column_t, high_ref, low_ref, stiff_high, stiff_low, x_ref, y_ref,
-    update_ref, residual_ref, inverse_ref, delta_ref, total_ref,
+    start_ref, loads_ref, nodes_ref, stiff_ref, arrive,
+    onehot, onehot_t, column_t, low_ref, high_ref, stiff_high, stiff_low, x_ref, y_ref,
+    start_table, update_ref, residual_ref, inverse_ref, delta_ref, total_ref,
     far_out, far_in, near_out, near_in, records, edge_out, edge_in,
     far_send, far_recv, near_send, near_recv, edge_send, edge_recv,
 ):
     per_element, slots = nodes_ref.shape
     dofs = loads_ref.shape[0]
     components = dofs // per_element
-    height = components * LOW
-    columns = owned // LOW
-    width = face // LOW
-    table = onehot.shape[1]
+    owned = start_ref.shape[1]
+    face = face_ref.shape[1]
+    height = start_table.shape[0]
+    depth = height // components
+    own_rows = owned // COLUMNS
+    edges = edge_out.shape[1]
     groups = per_element // GROUP
     me = lax.axis_index("seg") * subs + lax.axis_index("sub")
     has_prev = me > 0
     has_next = me < devices - 1
 
+    incoming = [
+        pltpu.make_async_copy(source, target, arrive.at[k])
+        for k, (source, target) in enumerate(
+            [(loads_hbm, loads_ref), (start_hbm, start_ref), (nodes_hbm, nodes_ref), (stiff_hbm, stiff_ref)]
+        )
+    ]
+    for copy in incoming:
+        copy.start()
+
     def coords(p):
         return {"seg": lax.div(p, subs), "sub": lax.rem(p, subs)}
 
@@ -120,7 +135,7 @@
 
     def edge_copy(way, t):
         return pltpu.make_async_remote_copy(
-            src_ref=edge_out.at[t], dst_ref=edge_in.at[way, t],
+            src_ref=edge_out.at[way, t], dst_ref=edge_in.at[way, t],
             send_sem=edge_send.at[way, t], recv_sem=edge_recv.at[way, t],
             device_id=after if way == 0 else before, device_id_type=pl.DeviceIdType.MESH,
         )
@@ -141,46 +156,87 @@
         def _():
             copies[1].start()
 
-    def finish(copies):
+    def receive(copies):
         @pl.when(has_prev)
         def _():
             copies[0].wait_recv()
-            copies[1].wait_send()
 
         @pl.when(has_next)
         def _():
             copies[1].wait_recv()
+
+    def sent(copies):
+        @pl.when(has_next)
+        def _():
             copies[0].wait_send()
 
+        @pl.when(has_prev)
+        def _():
+            copies[1].wait_send()
+
+    top = own_rows % TILE
+    tile_at = own_rows - top
+    sublane = lax.broadcasted_iota(i32, (TILE, LANES), 0)
+
     def send_edge(part, t):
-        edge_out[t] = part[:, table - LANES :]
+        for c in range(components):
+            at = c * depth + tile_at
+            left, right = part[at : at + TILE, :LANES], part[at : at + TILE, LANES:]
+            edge_out[0, t, c] = jnp.where(sublane == top + 2, pltpu.roll(right, 2, 0), left)
+            edge_out[1, t, c] = jnp.where(sublane == top, pltpu.roll(left, TILE - 2, 0), right)
         both_ways([edge_copy(0, t), edge_copy(1, t)])
 
-    lane = lax.broadcasted_iota(i32, (height, LANES), 1) - (columns - (table - LANES))
+    first_row, middle_row, last_row = (sublane == top + k for k in range(3))
 
     def receive_edge(part, t):
-        finish([edge_copy(0, t), edge_copy(1, t)])
-        from_prev = pltpu.roll(edge_in[0, t], 2 * width, 1)
-        from_next = pltpu.roll(edge_in[1, t], LANES - 2 * width, 1)
-        take_prev = (lane >= 2 * width) & (lane < 4 * width) & has_prev
-        take_next = (lane >= 0) & (lane < 2 * width) & has_next
-        tail = part[:, table - LANES :]
-        tail = tail + jnp.where(take_prev, from_prev, jnp.where(take_next, from_next, 0.0))
-        return jnp.concatenate([part[:, : table - LANES], tail], axis=1)
-
-    face_row = face_ref[...]
-    face_low = ((face_row.astype(f32) + 0.5) * (1.0 / columns)).astype(i32)
-    face_old = one_hot_rows(face_row - face_low * columns, table)
-    place = lax.broadcasted_iota(i32, face_row.shape, 1)
-    face_new_low = place & (LOW - 1)
-    face_new = one_hot_rows(lax.div(place, LOW) + columns + width, table)
-
-    start = jnp.concatenate(
-        [start_ref[...], jnp.zeros((height, table - columns), f32)], axis=1
-    )
-    face_values = pick_low(dot(jnp.concatenate(split(start), 0), face_old), face_low, components)
-    lifted = dot_nt(spread_low(face_values, face_new_low), face_new)
-    field = start + lifted[:height] + lifted[height:]
+        receive([edge_copy(0, t), edge_copy(1, t)])
+        pieces = []
+        for c in range(components):
+            at = c * depth + tile_at
+            left, right = part[at : at + TILE, :LANES], part[at : at + TILE, LANES:]
+            prev, next_ = edge_in[0, t, c], edge_in[1, t, c]
+            shifted = pltpu.roll(next_, TILE - 1, 0)
+            left = left + jnp.where(
+                last_row & has_prev, prev, jnp.where((first_row | middle_row) & has_next, shifted, 0.0)
+            )
+            shifted = pltpu.roll(prev, 1, 0)
+            right = right + jnp.where(
+                first_row & has_next, next_, jnp.where((middle_row | last_row) & has_prev, shifted, 0.0)
+            )
+            pieces += [
+                part[c * depth : at], jnp.concatenate([left, right], axis=1),
+                part[at + TILE : (c + 1) * depth],
+            ]
+        return jnp.concatenate([piece for piece in pieces if piece.shape[0]], axis=0)
+
+    lists = []
+    for k in range(2):
+        old = face_ref[1 - k : 2 - k, :]
+        new = owned + (1 + k) * face + lax.broadcasted_iota(i32, (1, face), 1)
+        lists.append(
+            [(node >> 8, one_hot_rows(node & (COLUMNS - 1), COLUMNS)) for node in (old, new)]
+        )
+
+    def move_faces(values, source, target):
+        both = jnp.concatenate(split(values), axis=0)
+        total = 0.0
+        for places in lists:
+            low, hot = places[source]
+            rows = pick_low(dot(both, hot), low, components)
+            low, hot = places[target]
+            total = total + dot_nt(spread_low(rows, low, depth), hot)
+        return total[:height] + total[height:]
+
+    incoming[0].wait()
+    incoming[1].wait()
+    start_table[...] = jnp.zeros_like(start_table)
+    for r in range(own_rows):
+        for c in range(components):
+            start_table[c * depth + r : c * depth + r + 1, :] = start_ref[
+                c : c + 1, r * COLUMNS : (r + 1) * COLUMNS
+            ]
+    start = start_table[...]
+    field = start + move_faces(start, 0, 1)
 
     dest = moves_ref[0:1, :]
     new_slot = moves_ref[1:2, :]
@@ -223,32 +279,31 @@
 
     lax.fori_loop(1, devices, far_start, 0)
 
+    incoming[2].wait()
     nodes = nodes_ref[...]
-    extra = jnp.where(
-        nodes < owned, -1, jnp.where(nodes < owned + face, nodes - owned + 3 * face, nodes - owned - face)
-    )
-
-    def relabel(s, extra):
-        extra = jnp.where(nodes == face_smem[1, s], face + s, extra)
-        return jnp.where(nodes == face_smem[0, s], 2 * face + s, extra)
-
-    extra = lax.fori_loop(0, face, relabel, extra, unroll=4)
-    own_low = ((nodes.astype(f32) + 0.5) * (1.0 / columns)).astype(i32)
-    low = jnp.where(extra >= 0, extra & (LOW - 1), own_low)
-    high = jnp.where(extra >= 0, columns + lax.div(extra, LOW), nodes - own_low * columns)
-    high_ref[...] = high
-    low_ref[...] = low
-    high_t = jnp.transpose(high.astype(f32)).astype(i32)
+    place = jnp.where(
+        nodes < owned, nodes, jnp.where(nodes < owned + face, nodes + 3 * face, nodes - face)
+    )
+
+    def relabel(s, place):
+        place = jnp.where(nodes == face_smem[1, s], owned + face + s, place)
+        return jnp.where(nodes == face_smem[0, s], owned + 2 * face + s, place)
+
+    place = lax.fori_loop(0, face, relabel, place, unroll=8)
+    low_ref[...] = place >> 8
+    column = place & (COLUMNS - 1)
+    high_ref[...] = column
+    column_rows = jnp.transpose(column.astype(f32)).astype(i32)
     for g in range(groups):
-        column_t[g] = high_t[:, g * GROUP : (g + 1) * GROUP]
+        column_t[g] = column_rows[:, g * GROUP : (g + 1) * GROUP]
 
     def build(g, _):
         own = column_t[g]
         rows8 = high_ref[pl.ds(pl.multiple_of(g * GROUP, GROUP), GROUP), :]
         for j in range(GROUP):
             n = g * GROUP + j
-            onehot[n] = one_hot_rows(rows8[j : j + 1], table)
-            hit = lax.broadcasted_iota(i32, (slots, table), 1) == own[:, j : j + 1]
+            onehot[n] = one_hot_rows(rows8[j : j + 1], COLUMNS)
+            hit = lax.broadcasted_iota(i32, (slots, COLUMNS), 1) == own[:, j : j + 1]
             onehot_t[pl.ds(pl.multiple_of(n * slots, slots), slots), :] = jnp.where(
                 hit, 1.0, 0.0
             ).astype(bf16)
@@ -256,6 +311,7 @@
 
     lax.fori_loop(0, groups, build, 0)
 
+    incoming[3].wait()
     stiff = stiff_ref[...]
     stiff_high[...] = stiff.astype(bf16)
     stiff_low[...] = (stiff - stiff_high[...].astype(f32)).astype(bf16)
@@ -275,7 +331,7 @@
                 x_ref[pl.ds(at, GROUP), :] = jnp.concatenate(found[c], axis=0)
             return 0
 
-        lax.fori_loop(0, groups, step, 0)
+        lax.fori_loop(0, groups, step, 0, unroll=UNROLL)
 
     def scatter(values):
         y_ref[...] = values
@@ -289,7 +345,7 @@
             ]
             wide = jnp.concatenate(
                 [
-                    spread_low([part[j : j + 1] for part in parts], low8[j : j + 1])
+                    spread_low([part[j : j + 1] for part in parts], low8[j : j + 1], depth)
                     for j in range(GROUP)
                 ],
                 axis=1,
@@ -298,7 +354,7 @@
             total_ref[...] += dot(wide, onehot_t[pl.ds(at, GROUP * slots), :])
             return 0
 
-        lax.fori_loop(0, groups, step, 0)
+        lax.fori_loop(0, groups, step, 0, unroll=UNROLL)
         return total_ref[:height] + total_ref[height:]
 
     def products():
@@ -311,12 +367,11 @@
     gather(field)
     both = products()
 
-    finish([near_copy(0), near_copy(1)])
+    receive([near_copy(0), near_copy(1)])
 
     def far_finish(d, _):
         p = lax.rem(me + d, devices)
         far_copy(p, p).wait_recv()
-        far_copy(p, p).wait_send()
         return 0
 
     lax.fori_loop(1, devices, far_finish, 0)
@@ -380,12 +435,26 @@
     lax.fori_loop(0, len(weights), sweep_step, 0)
 
     delta = delta_ref[...] + update_ref[...]
-    face_values = pick_low(
-        dot(jnp.concatenate(split(delta), 0), face_new), face_new_low, components
-    )
-    lowered = dot_nt(spread_low(face_values, face_low), face_old)
-    result = start + delta + lowered[:height] + lowered[height:]
-    out_ref[...] = result[:, :columns]
+    result = start_table[...] + delta + move_faces(delta, 1, 0)
+    for r in range(own_rows):
+        for c in range(components):
+            out_ref[c : c + 1, r * COLUMNS : (r + 1) * COLUMNS] = result[
+                c * depth + r : c * depth + r + 1
+            ]
+
+    sent([near_copy(0), near_copy(1)])
+
+    def far_sent(d, _):
+        far_copy(lax.rem(me + d, devices), me).wait_send()
+        return 0
+
+    lax.fori_loop(1, devices, far_sent, 0)
+
+    def edge_sent(t, _):
+        sent([edge_copy(0, t), edge_copy(1, t)])
+        return 0
+
+    lax.fori_loop(0, edges, edge_sent, 0)
 
 
 def local(
@@ -397,27 +466,34 @@
     components = dofs // per_element
     owned = start_field.shape[1]
     face = face_nodes.shape[1]
-    height = components * LOW
-    columns = owned // LOW
-    table = -(-(columns + 4 * (face // LOW)) // LANES) * LANES
+    extra_rows = 4 * face // COLUMNS
+    own_rows = owned // COLUMNS
+    assert owned % COLUMNS == 0 and 4 * face == 3 * COLUMNS and own_rows % TILE + 3 <= TILE
+    depth = -(-(own_rows + extra_rows) // TILE) * TILE
+    table = (components * depth, COLUMNS)
     groups = per_element // GROUP
     rows = -(-(devices + 2 * NEAR_CAP) // LANES) * LANES
     edges = 2 + SWEEPS * DEGREE
     vmem = pl.BlockSpec(memory_space=pltpu.VMEM)
     smem = pl.BlockSpec(memory_space=pltpu.SMEM)
-    wide = (height, table)
-    smoothed, moved_loads, moved_coefs = pl.pallas_call(
-        functools.partial(kernel, devices, subs, owned, face),
+    anywhere = pl.BlockSpec(memory_space=pl.ANY)
+    return pl.pallas_call(
+        functools.partial(kernel, devices, subs),
         out_shape=(
-            jax.ShapeDtypeStruct((height, columns), f32),
+            jax.ShapeDtypeStruct(start_field.shape, f32),
             jax.ShapeDtypeStruct((dofs, slots), f32),
             jax.ShapeDtypeStruct((2, slots), f32),
         ),
-        in_specs=[vmem] * 5 + [smem, vmem, vmem],
+        in_specs=[anywhere, anywhere, vmem, anywhere, vmem, smem, vmem, anywhere],
         out_specs=(vmem, vmem, vmem),
         scratch_shapes=[
-            pltpu.VMEM((per_element, table, slots), bf16),
-            pltpu.VMEM((per_element * slots, table), bf16),
+            pltpu.VMEM(start_field.shape, f32),
+            pltpu.VMEM((dofs, slots), f32),
+            pltpu.VMEM((per_element, slots), i32),
+            pltpu.VMEM((2 * dofs, dofs), f32),
+            pltpu.SemaphoreType.DMA((4,)),
+            pltpu.VMEM((per_element, COLUMNS, slots), bf16),
+            pltpu.VMEM((per_element * slots, COLUMNS), bf16),
             pltpu.VMEM((groups, slots, GROUP), i32),
             pltpu.VMEM((per_element, slots), i32),
             pltpu.VMEM((per_element, slots), i32),
@@ -425,18 +501,19 @@
             pltpu.VMEM((2 * dofs, dofs), bf16),
             pltpu.VMEM((dofs, slots), f32),
             pltpu.VMEM((dofs, slots), f32),
-            pltpu.VMEM(wide, f32),
-            pltpu.VMEM(wide, f32),
-            pltpu.VMEM(wide, f32),
-            pltpu.VMEM(wide, f32),
-            pltpu.VMEM((2 * height, table), f32),
+            pltpu.VMEM(table, f32),
+            pltpu.VMEM(table, f32),
+            pltpu.VMEM(table, f32),
+            pltpu.VMEM(table, f32),
+            pltpu.VMEM(table, f32),
+            pltpu.VMEM((2 * table[0], COLUMNS), f32),
             pltpu.VMEM((devices, 1, slots), f32),
             pltpu.VMEM((devices, 1, slots), f32),
             pltpu.VMEM((2, NEAR_CAP, slots), f32),
             pltpu.VMEM((2, NEAR_CAP, slots), f32),
             pltpu.VMEM((rows, slots), f32),
-            pltpu.VMEM((edges, height, LANES), f32),
-            pltpu.VMEM((2, edges, height, LANES), f32),
+            pltpu.VMEM((2, edges, components, TILE, LANES), f32),
+            pltpu.VMEM((2, edges, components, TILE, LANES), f32),
             pltpu.SemaphoreType.DMA((devices,)),
             pltpu.SemaphoreType.DMA((devices,)),
             pltpu.SemaphoreType.DMA((2,)),
@@ -445,20 +522,19 @@
             pltpu.SemaphoreType.DMA((2, edges)),
         ],
         compiler_params=pltpu.CompilerParams(
-            collective_id=0, has_side_effects=True, vmem_limit_bytes=48 * 1024 * 1024
+            collective_id=0, has_side_effects=True, vmem_limit_bytes=56 * 1024 * 1024
         ),
         name="migrate_and_smooth",
     )(
-        start_field.reshape(height, columns),
+        start_field,
         element_loads,
         element_coefs,
         element_nodes,
         move_list,
         face_nodes,
-        jnp.concatenate([face_nodes[1], face_nodes[0]])[None, :],
+        face_nodes,
         stiffness.reshape(2 * dofs, dofs),
     )
-    return smoothed.reshape(components, owned), moved_loads, moved_coefs
 
 
 def solution(mesh):

time: 107 us -> 83.7 us (0.78)
  Pallas kernels: 100 us -> 80 us
  local copies, waits for them, and re-layouts: 5.75 us -> 2.86 us
    pallas_call x1, Pallas kernels: 100 us -> 80 us  [local(): pl.pallas_call(functools.partial(kernel, devices, subs), out_shape=(jax.S...]
    reshape x2 -> x0, local copies, waits for them, and re-layouts: 1.89 us -> none  [the longest x1 1.09 us: local(): start_field.reshape(height, columns)]
    unnamed x14 -> x7, local copies, waits for them, and re-layouts: 3.1 us -> 2.86 us
where the time goes in v2:
time: 83.7 us; the launch traced here: 83.5 us
  Pallas kernels  80 us (96%)
  local copies, waits for them, and re-layouts  2.86 us (3%)
    pallas_call x1, Pallas kernels, local(): pl.pallas_call(functools.partial(kernel, devices, subs), out_shape=(jax.S...  80 us
    unnamed x7, local copies, waits for them, and re-layouts  2.86 us

profile of v2, /device:TPU:8, one launch (start us, length us, event | category | flops | bytes accessed | tf_op | source)
XLA Modules:
  0.0 83.5 jit_solution(12123060721122190331)
XLA Ops:
  0.6 80.0 %migrate_and_smooth.1 = (f32[3,6912]{1,0:T(4,128)}, f32[192,256]{1,0:T(8,128)}, f32[2,256]{1,0:T(2,128)}) custom-call(f32[3,6912]{1,0:T(4,128)} %start_hbm.1, f32[192,256]{1,0:T(8,128)} %loads_hbm.1, f32[2,256]{1,0:T(2,128)} %coefs_ref.1, s32[64,256]{1,0:T(8,128)} %nodes_hbm.1, s32[3,256]{1,0:T(4,128)} %moves_ref.1, s32[2,192]{1,0:T(2,128)} %face_ref.1, ...), custom_call_target="tpu_custom_call" | custom-call | tf_op jit(solution)/shard_map/migrate_and_smooth/pallas_call | solution.py:480
  80.7 0.0 copy-start
  80.7 1.6 %copy.13 = f32[3,6912]{1,0:T(4,128)} copy(f32[3,6912]{1,0:T(4,128)} %get-tuple-element.6) | data formatting | bytes 165888
  82.3 0.0 copy-done
  82.3 0.0 copy-start.1
  82.3 0.7 copy.14
  83.0 0.0 copy-done.1
  83.0 0.6 copy.15
Async XLA Ops:
  80.7 1.6 %copy-start = (f32[192,256]{1,0:T(8,128)S(1)}, f32[192,256]{1,0:T(8,128)}, u32[]{:S(2)}) copy-start(f32[192,256]{1,0:T(8,128)} %get-tuple-element.7) | copy-start | bytes 589828
  82.3 0.7 copy-start.1

commit v3 on v2

--- a/solution.py
+++ b/solution.py
@@ -28,9 +28,8 @@
 def chebyshev_weights():
     weights = []
     scaled_center = center / half_width
-    for sweep_index in range(SWEEPS):
-        if sweep_index:
-            weights.append((0.0, 1.0 / center))
+    for _ in range(SWEEPS):
+        weights.append((0.0, 1.0 / center))
         ratio = 1.0 / scaled_center
         for _ in range(DEGREE - 1):
             ratio_next = 1.0 / (2.0 * scaled_center - ratio)
@@ -77,8 +76,9 @@
 
 
 def one_hot_rows(row, count):
-    hit = lax.broadcasted_iota(i32, (count, row.shape[1]), 0) == row
-    return jnp.where(hit, 1.0, 0.0).astype(bf16)
+    numbers = lax.broadcasted_iota(i32, (count, row.shape[1]), 0).astype(f32).astype(bf16)
+    hit = numbers == row.astype(f32).astype(bf16)
+    return jnp.where(hit, jnp.ones_like(numbers), jnp.zeros_like(numbers))
 
 
 def kernel(
@@ -86,8 +86,8 @@
     start_hbm, loads_hbm, coefs_ref, nodes_hbm, moves_ref, face_smem, face_ref, stiff_hbm,
     out_ref, moved_loads_ref, moved_coefs_ref,
     start_ref, loads_ref, nodes_ref, stiff_ref, arrive,
-    onehot, onehot_t, column_t, low_ref, high_ref, stiff_high, stiff_low, x_ref, y_ref,
-    start_table, update_ref, residual_ref, inverse_ref, delta_ref, total_ref,
+    onehot, onehot_t, column_t, low_ref, high_ref, extra_ref, stiff_high, stiff_low, x_ref, y_ref,
+    start_table, update_ref, residual_ref, inverse_ref, delta_ref, part_ref, total_ref,
     far_out, far_in, near_out, near_in, records, edge_out, edge_in,
     far_send, far_recv, near_send, near_recv, edge_send, edge_recv,
 ):
@@ -293,20 +293,22 @@
     low_ref[...] = place >> 8
     column = place & (COLUMNS - 1)
     high_ref[...] = column
-    column_rows = jnp.transpose(column.astype(f32)).astype(i32)
+    extra_ref[...] = place - owned
+    column_rows = jnp.transpose(column.astype(f32))
     for g in range(groups):
         column_t[g] = column_rows[:, g * GROUP : (g + 1) * GROUP]
 
     def build(g, _):
-        own = column_t[g]
+        own = column_t[g].astype(bf16)
+        numbers = lax.broadcasted_iota(i32, (slots, COLUMNS), 1).astype(f32).astype(bf16)
         rows8 = high_ref[pl.ds(pl.multiple_of(g * GROUP, GROUP), GROUP), :]
         for j in range(GROUP):
             n = g * GROUP + j
             onehot[n] = one_hot_rows(rows8[j : j + 1], COLUMNS)
-            hit = lax.broadcasted_iota(i32, (slots, COLUMNS), 1) == own[:, j : j + 1]
+            hit = numbers == own[:, j : j + 1]
             onehot_t[pl.ds(pl.multiple_of(n * slots, slots), slots), :] = jnp.where(
-                hit, 1.0, 0.0
-            ).astype(bf16)
+                hit, jnp.ones_like(numbers), jnp.zeros_like(numbers)
+            )
         return 0
 
     lax.fori_loop(0, groups, build, 0)
@@ -332,6 +334,23 @@
             return 0
 
         lax.fori_loop(0, groups, step, 0, unroll=UNROLL)
+
+    def gather_interface(values):
+        for side in range(slots // LANES):
+            lanes = slice(side * LANES, (side + 1) * LANES)
+            extra = extra_ref[:, lanes]
+            lane_of = extra & (LANES - 1)
+            piece_of = extra >> 7
+            for c in range(components):
+                rows = slice(c * per_element, (c + 1) * per_element)
+                found = x_ref[rows, lanes]
+                for piece in range(4 * face // LANES):
+                    r = c * depth + own_rows + piece // 2
+                    line = values[r : r + 1, (piece % 2) * LANES : (piece % 2 + 1) * LANES]
+                    line = jnp.broadcast_to(line, (per_element, LANES))
+                    taken = jnp.take_along_axis(line, lane_of, axis=1, mode="promise_in_bounds")
+                    found = found + jnp.where(piece_of == piece, taken, 0.0)
+                x_ref[rows, lanes] = found
 
     def scatter(values):
         y_ref[...] = values
@@ -363,8 +382,8 @@
             dot(stiff_low[...], x_high) + dot(stiff_high[...], x_low)
         )
 
-    field = receive_edge(field, 0)
-    gather(field)
+    gather(start_table[...])
+    gather_interface(receive_edge(field, 0))
     both = products()
 
     receive([near_copy(0), near_copy(1)])
@@ -404,37 +423,45 @@
         jnp.sum(jnp.where(on_diagonal, stiff[k * dofs : (k + 1) * dofs], 0.0), axis=1, keepdims=True)
         for k in range(2)
     ]
-    part = scatter(loads - element_values(both))
-    send_edge(part, 1)
     diagonal = scatter(diagonals[0] * first + diagonals[1] * second)
-    send_edge(diagonal, 2)
-    residual = receive_edge(part, 1)
-    diagonal = receive_edge(diagonal, 2)
-    inverse = jnp.where(diagonal > 0.0, 1.0 / diagonal, 0.0)
-    inverse_ref[...] = inverse
-    residual_ref[...] = residual
-    update_ref[...] = residual * inverse * (1.0 / center)
+    send_edge(diagonal, 1)
+    part = scatter(element_values(both) - loads)
+    send_edge(part, 2)
+    part_ref[...] = part
+    diagonal = receive_edge(diagonal, 1)
+    inverse_ref[...] = jnp.where(diagonal > 0.0, 1.0 / diagonal, 0.0)
+    residual_ref[...] = jnp.zeros_like(residual_ref)
+    update_ref[...] = jnp.zeros_like(update_ref)
     delta_ref[...] = jnp.zeros_like(delta_ref)
     weights = chebyshev_weights()
+    table_row = lax.broadcasted_iota(i32, (height, COLUMNS), 0)
+    is_owned = lax.rem(table_row, depth) < own_rows
+
+    def next_update(part, old, new):
+        residual = residual_ref[...] - part
+        return residual, old * update_ref[...] + new * (residual * inverse_ref[...])
 
     def sweep_step(i, _):
-        update = update_ref[...]
+        old, new = jnp.float32(0.0), jnp.float32(0.0)
+        for k, (a, b) in enumerate(weights[:-1]):
+            old = jnp.where(i == k, a, old)
+            new = jnp.where(i == k, b, new)
+        part = part_ref[...]
+        gather(jnp.where(is_owned, next_update(part, old, new)[1], 0.0))
+        residual, update = next_update(receive_edge(part, 2 + i), old, new)
+        residual_ref[...] = residual
+        update_ref[...] = update
         delta_ref[...] += update
-        gather(update)
+        gather_interface(update)
         part = scatter(element_values(products()))
         send_edge(part, 3 + i)
-        residual = residual_ref[...] - receive_edge(part, 3 + i)
-        residual_ref[...] = residual
-        old, new = jnp.float32(0.0), jnp.float32(0.0)
-        for k, (a, b) in enumerate(weights):
-            old = jnp.where(i == k, a, old)
-            new = jnp.where(i == k, b, new)
-        update_ref[...] = old * update + new * (residual * inverse_ref[...])
-        return 0
-
-    lax.fori_loop(0, len(weights), sweep_step, 0)
-
-    delta = delta_ref[...] + update_ref[...]
+        part_ref[...] = part
+        return 0
+
+    lax.fori_loop(0, len(weights) - 1, sweep_step, 0)
+
+    part = receive_edge(part_ref[...], 1 + len(weights))
+    delta = delta_ref[...] + next_update(part, *weights[-1])[1]
     result = start_table[...] + delta + move_faces(delta, 1, 0)
     for r in range(own_rows):
         for c in range(components):
@@ -494,13 +521,15 @@
             pltpu.SemaphoreType.DMA((4,)),
             pltpu.VMEM((per_element, COLUMNS, slots), bf16),
             pltpu.VMEM((per_element * slots, COLUMNS), bf16),
-            pltpu.VMEM((groups, slots, GROUP), i32),
+            pltpu.VMEM((groups, slots, GROUP), f32),
+            pltpu.VMEM((per_element, slots), i32),
             pltpu.VMEM((per_element, slots), i32),
             pltpu.VMEM((per_element, slots), i32),
             pltpu.VMEM((2 * dofs, dofs), bf16),
             pltpu.VMEM((2 * dofs, dofs), bf16),
             pltpu.VMEM((dofs, slots), f32),
             pltpu.VMEM((dofs, slots), f32),
+            pltpu.VMEM(table, f32),
             pltpu.VMEM(table, f32),
             pltpu.VMEM(table, f32),
             pltpu.VMEM(table, f32),

time: 83.7 us -> 73.6 us (0.88)
  Pallas kernels: 80 us -> 69.9 us
    pallas_call x1, Pallas kernels: 80 us -> 69.9 us  [local(): pl.pallas_call(functools.partial(kernel, devices, subs), out_shape=(jax.S...]
where the time goes in v3:
time: 73.6 us; the launch traced here: 73.4 us
  Pallas kernels  69.9 us (95%)
  local copies, waits for them, and re-layouts  2.86 us (4%)
    pallas_call x1, Pallas kernels, local(): pl.pallas_call(functools.partial(kernel, devices, subs), out_shape=(jax.S...  69.9 us
    unnamed x7, local copies, waits for them, and re-layouts  2.86 us

profile of v3, /device:TPU:8, one launch (start us, length us, event | category | flops | bytes accessed | tf_op | source)
XLA Modules:
  0.0 73.4 jit_solution(12528534157696622578)
XLA Ops:
  0.6 69.9 %migrate_and_smooth.1 = (f32[3,6912]{1,0:T(4,128)}, f32[192,256]{1,0:T(8,128)}, f32[2,256]{1,0:T(2,128)}) custom-call(f32[3,6912]{1,0:T(4,128)} %start_hbm.1, f32[192,256]{1,0:T(8,128)} %loads_hbm.1, f32[2,256]{1,0:T(2,128)} %coefs_ref.1, s32[64,256]{1,0:T(8,128)} %nodes_hbm.1, s32[3,256]{1,0:T(4,128)} %moves_ref.1, s32[2,192]{1,0:T(2,128)} %face_ref.1, ...), custom_call_target="tpu_custom_call" | custom-call | tf_op jit(solution)/shard_map/migrate_and_smooth/pallas_call | solution.py:507
  70.5 0.0 copy-start
  70.5 1.6 %copy.13 = f32[3,6912]{1,0:T(4,128)} copy(f32[3,6912]{1,0:T(4,128)} %get-tuple-element.6) | data formatting | bytes 165888
  72.1 0.0 copy-done
  72.1 0.0 copy-start.1
  72.1 0.7 copy.14
  72.8 0.0 copy-done.1
  72.8 0.6 copy.15
Async XLA Ops:
  70.5 1.6 %copy-start = (f32[192,256]{1,0:T(8,128)S(1)}, f32[192,256]{1,0:T(8,128)}, u32[]{:S(2)}) copy-start(f32[192,256]{1,0:T(8,128)} %get-tuple-element.7) | copy-start | bytes 589828
  72.1 0.7 copy-start.1

commit v4 on v3

--- a/solution.py
+++ b/solution.py
@@ -15,6 +15,7 @@
 GROUP = 8
 LANES = 128
 UNROLL = 4
+GATHER_UNROLL = 3
 
 center = 1.125
 half_width = 0.875
@@ -64,8 +65,8 @@
     ]
 
 
-def spread_low(rows, low_row, depth):
-    mask = lax.broadcasted_iota(i32, (depth, low_row.shape[1]), 0) == low_row
+def spread_low(rows, low_row, first, last):
+    mask = lax.broadcasted_iota(i32, (last - first, low_row.shape[1]), 0) == low_row - first
     tall = []
     for part in range(2):
         for row in rows:
@@ -86,8 +87,8 @@
     start_hbm, loads_hbm, coefs_ref, nodes_hbm, moves_ref, face_smem, face_ref, stiff_hbm,
     out_ref, moved_loads_ref, moved_coefs_ref,
     start_ref, loads_ref, nodes_ref, stiff_ref, arrive,
-    onehot, onehot_t, column_t, low_ref, high_ref, extra_ref, stiff_high, stiff_low, x_ref, y_ref,
-    start_table, update_ref, residual_ref, inverse_ref, delta_ref, part_ref, total_ref,
+    onehot_t, column_t, low_ref, place_ref, stiff_high, stiff_low, x_ref, y_ref,
+    start_table, update_ref, residual_ref, inverse_ref, delta_ref, part_ref, early_ref, total_ref,
     far_out, far_in, near_out, near_in, records, edge_out, edge_in,
     far_send, far_recv, near_send, near_recv, edge_send, edge_recv,
 ):
@@ -180,7 +181,7 @@
 
     def send_edge(part, t):
         for c in range(components):
-            at = c * depth + tile_at
+            at = c * TILE
             left, right = part[at : at + TILE, :LANES], part[at : at + TILE, LANES:]
             edge_out[0, t, c] = jnp.where(sublane == top + 2, pltpu.roll(right, 2, 0), left)
             edge_out[1, t, c] = jnp.where(sublane == top, pltpu.roll(left, TILE - 2, 0), right)
@@ -224,7 +225,7 @@
             low, hot = places[source]
             rows = pick_low(dot(both, hot), low, components)
             low, hot = places[target]
-            total = total + dot_nt(spread_low(rows, low, depth), hot)
+            total = total + dot_nt(spread_low(rows, low, 0, depth), hot)
         return total[:height] + total[height:]
 
     incoming[0].wait()
@@ -270,7 +271,12 @@
         )
 
     pl.semaphore_wait(barrier, devices - 1)
-    send_edge(field, 0)
+    send_edge(
+        jnp.concatenate(
+            [field[c * depth + tile_at : (c + 1) * depth] for c in range(components)], axis=0
+        ),
+        0,
+    )
     both_ways([near_copy(0), near_copy(1)])
 
     def far_start(d, _):
@@ -292,8 +298,7 @@
     place = lax.fori_loop(0, face, relabel, place, unroll=8)
     low_ref[...] = place >> 8
     column = place & (COLUMNS - 1)
-    high_ref[...] = column
-    extra_ref[...] = place - owned
+    place_ref[...] = place
     column_rows = jnp.transpose(column.astype(f32))
     for g in range(groups):
         column_t[g] = column_rows[:, g * GROUP : (g + 1) * GROUP]
@@ -301,10 +306,8 @@
     def build(g, _):
         own = column_t[g].astype(bf16)
         numbers = lax.broadcasted_iota(i32, (slots, COLUMNS), 1).astype(f32).astype(bf16)
-        rows8 = high_ref[pl.ds(pl.multiple_of(g * GROUP, GROUP), GROUP), :]
         for j in range(GROUP):
             n = g * GROUP + j
-            onehot[n] = one_hot_rows(rows8[j : j + 1], COLUMNS)
             hit = numbers == own[:, j : j + 1]
             onehot_t[pl.ds(pl.multiple_of(n * slots, slots), slots), :] = jnp.where(
                 hit, jnp.ones_like(numbers), jnp.zeros_like(numbers)
@@ -318,43 +321,43 @@
     stiff_high[...] = stiff.astype(bf16)
     stiff_low[...] = (stiff - stiff_high[...].astype(f32)).astype(bf16)
 
-    def gather(values):
-        both = jnp.concatenate(split(values), axis=0)
-
-        def step(g, _):
-            low8 = low_ref[pl.ds(pl.multiple_of(g * GROUP, GROUP), GROUP), :]
-            found = [[] for _ in range(components)]
-            for j in range(GROUP):
-                rows = pick_low(dot(both, onehot[g * GROUP + j]), low8[j : j + 1], components)
-                for c in range(components):
-                    found[c].append(rows[c])
-            for c in range(components):
-                at = pl.multiple_of(c * per_element + g * GROUP, GROUP)
-                x_ref[pl.ds(at, GROUP), :] = jnp.concatenate(found[c], axis=0)
-            return 0
-
-        lax.fori_loop(0, groups, step, 0, unroll=UNROLL)
-
-    def gather_interface(values):
+    def gather(table_ref, first, last, found_of, unroll):
         for side in range(slots // LANES):
             lanes = slice(side * LANES, (side + 1) * LANES)
-            extra = extra_ref[:, lanes]
-            lane_of = extra & (LANES - 1)
-            piece_of = extra >> 7
+            place = place_ref[:, lanes]
+            lane_of = place & (LANES - 1)
+            piece_of = place >> 7
+
+            def step(r, found):
+                lines = [table_ref[pl.ds(c * depth + r, 1), :] for c in range(components)]
+                for half in range(2):
+                    hit = piece_of == 2 * r + half
+                    taken = []
+                    for c in range(components):
+                        line = lines[c][:, half * LANES : (half + 1) * LANES]
+                        line = jnp.broadcast_to(line, (per_element, LANES))
+                        line = jnp.take_along_axis(line, lane_of, axis=1, mode="promise_in_bounds")
+                        taken.append(jnp.where(hit, line, found[c]))
+                    found = tuple(taken)
+                return found
+
+            rows = [slice(c * per_element, (c + 1) * per_element) for c in range(components)]
+            found = tuple(found_of(row, lanes) for row in rows)
+            found = lax.fori_loop(first, last, step, found, unroll=unroll)
             for c in range(components):
-                rows = slice(c * per_element, (c + 1) * per_element)
-                found = x_ref[rows, lanes]
-                for piece in range(4 * face // LANES):
-                    r = c * depth + own_rows + piece // 2
-                    line = values[r : r + 1, (piece % 2) * LANES : (piece % 2 + 1) * LANES]
-                    line = jnp.broadcast_to(line, (per_element, LANES))
-                    taken = jnp.take_along_axis(line, lane_of, axis=1, mode="promise_in_bounds")
-                    found = found + jnp.where(piece_of == piece, taken, 0.0)
-                x_ref[rows, lanes] = found
-
-    def scatter(values):
-        y_ref[...] = values
-        total_ref[...] = jnp.zeros_like(total_ref)
+                x_ref[rows[c], lanes] = found[c]
+
+    def gather_owned(table_ref):
+        gather(
+            table_ref, 0, own_rows, lambda row, lanes: jnp.zeros((per_element, LANES), f32), GATHER_UNROLL
+        )
+
+    def gather_interface(table_ref):
+        gather(table_ref, own_rows, own_rows + 3, lambda row, lanes: x_ref[row, lanes], True)
+
+    def scatter_rows(first, last):
+        count = 2 * components * (last - first)
+        total_ref[:count] = jnp.zeros((count, COLUMNS), f32)
 
         def step(g, _):
             low8 = low_ref[pl.ds(pl.multiple_of(g * GROUP, GROUP), GROUP), :]
@@ -364,17 +367,27 @@
             ]
             wide = jnp.concatenate(
                 [
-                    spread_low([part[j : j + 1] for part in parts], low8[j : j + 1], depth)
+                    spread_low([part[j : j + 1] for part in parts], low8[j : j + 1], first, last)
                     for j in range(GROUP)
                 ],
                 axis=1,
             )
             at = pl.multiple_of(g * GROUP * slots, GROUP * slots)
-            total_ref[...] += dot(wide, onehot_t[pl.ds(at, GROUP * slots), :])
+            total_ref[:count] += dot(wide, onehot_t[pl.ds(at, GROUP * slots), :])
             return 0
 
         lax.fori_loop(0, groups, step, 0, unroll=UNROLL)
-        return total_ref[:height] + total_ref[height:]
+        return total_ref[: count // 2] + total_ref[count // 2 : count]
+
+    def scatter(values, t):
+        y_ref[...] = values
+        edge = scatter_rows(tile_at, depth)
+        send_edge(edge, t)
+        rest = scatter_rows(0, tile_at)
+        pieces = []
+        for c in range(components):
+            pieces += [rest[c * tile_at : (c + 1) * tile_at], edge[c * TILE : (c + 1) * TILE]]
+        return jnp.concatenate(pieces, axis=0)
 
     def products():
         x_high, x_low = split(x_ref[...])
@@ -382,8 +395,9 @@
             dot(stiff_low[...], x_high) + dot(stiff_high[...], x_low)
         )
 
-    gather(start_table[...])
-    gather_interface(receive_edge(field, 0))
+    gather_owned(start_table)
+    update_ref[...] = receive_edge(field, 0)
+    gather_interface(update_ref)
     both = products()
 
     receive([near_copy(0), near_copy(1)])
@@ -423,19 +437,14 @@
         jnp.sum(jnp.where(on_diagonal, stiff[k * dofs : (k + 1) * dofs], 0.0), axis=1, keepdims=True)
         for k in range(2)
     ]
-    diagonal = scatter(diagonals[0] * first + diagonals[1] * second)
-    send_edge(diagonal, 1)
-    part = scatter(element_values(both) - loads)
-    send_edge(part, 2)
-    part_ref[...] = part
+    diagonal = scatter(diagonals[0] * first + diagonals[1] * second, 1)
+    part_ref[...] = scatter(element_values(both) - loads, 2)
     diagonal = receive_edge(diagonal, 1)
     inverse_ref[...] = jnp.where(diagonal > 0.0, 1.0 / diagonal, 0.0)
     residual_ref[...] = jnp.zeros_like(residual_ref)
     update_ref[...] = jnp.zeros_like(update_ref)
     delta_ref[...] = jnp.zeros_like(delta_ref)
     weights = chebyshev_weights()
-    table_row = lax.broadcasted_iota(i32, (height, COLUMNS), 0)
-    is_owned = lax.rem(table_row, depth) < own_rows
 
     def next_update(part, old, new):
         residual = residual_ref[...] - part
@@ -447,15 +456,14 @@
             old = jnp.where(i == k, a, old)
             new = jnp.where(i == k, b, new)
         part = part_ref[...]
-        gather(jnp.where(is_owned, next_update(part, old, new)[1], 0.0))
+        early_ref[...] = next_update(part, old, new)[1]
+        gather_owned(early_ref)
         residual, update = next_update(receive_edge(part, 2 + i), old, new)
         residual_ref[...] = residual
         update_ref[...] = update
         delta_ref[...] += update
-        gather_interface(update)
-        part = scatter(element_values(products()))
-        send_edge(part, 3 + i)
-        part_ref[...] = part
+        gather_interface(update_ref)
+        part_ref[...] = scatter(element_values(products()), 3 + i)
         return 0
 
     lax.fori_loop(0, len(weights) - 1, sweep_step, 0)
@@ -519,16 +527,15 @@
             pltpu.VMEM((per_element, slots), i32),
             pltpu.VMEM((2 * dofs, dofs), f32),
             pltpu.SemaphoreType.DMA((4,)),
-            pltpu.VMEM((per_element, COLUMNS, slots), bf16),
             pltpu.VMEM((per_element * slots, COLUMNS), bf16),
             pltpu.VMEM((groups, slots, GROUP), f32),
-            pltpu.VMEM((per_element, slots), i32),
             pltpu.VMEM((per_element, slots), i32),
             pltpu.VMEM((per_element, slots), i32),
             pltpu.VMEM((2 * dofs, dofs), bf16),
             pltpu.VMEM((2 * dofs, dofs), bf16),
             pltpu.VMEM((dofs, slots), f32),
             pltpu.VMEM((dofs, slots), f32),
+            pltpu.VMEM(table, f32),
             pltpu.VMEM(table, f32),
             pltpu.VMEM(table, f32),
             pltpu.VMEM(table, f32),

time: 73.6 us -> 127 us (1.73); the launches traced: 73.4 us -> 125 us
  Pallas kernels: 69.9 us -> 121 us
    pallas_call x1, Pallas kernels: 69.9 us -> 121 us  [local(): pl.pallas_call(functools.partial(kernel, devices, subs), out_shape=(jax.S...]
where the time goes in v4:
time: 127 us; the launch traced here: 125 us
  Pallas kernels  121 us (95%)
  local copies, waits for them, and re-layouts  2.86 us (2%)
    pallas_call x1, Pallas kernels, local(): pl.pallas_call(functools.partial(kernel, devices, subs), out_shape=(jax.S...  121 us
    unnamed x7, local copies, waits for them, and re-layouts  2.86 us

profile of v4, /device:TPU:8, one launch (start us, length us, event | category | flops | bytes accessed | tf_op | source)
XLA Modules:
  0.0 125.0 jit_solution(16903642057690253626)
XLA Ops:
  0.6 121.5 %migrate_and_smooth.1 = (f32[3,6912]{1,0:T(4,128)}, f32[192,256]{1,0:T(8,128)}, f32[2,256]{1,0:T(2,128)}) custom-call(f32[3,6912]{1,0:T(4,128)} %start_hbm.1, f32[192,256]{1,0:T(8,128)} %loads_hbm.1, f32[2,256]{1,0:T(2,128)} %coefs_ref.1, s32[64,256]{1,0:T(8,128)} %nodes_hbm.1, s32[3,256]{1,0:T(4,128)} %moves_ref.1, s32[2,192]{1,0:T(2,128)} %face_ref.1, ...), custom_call_target="tpu_custom_call" | custom-call | tf_op jit(solution)/shard_map/migrate_and_smooth/pallas_call | solution.py:515
  122.1 0.0 copy-start
  122.1 1.6 %copy.13 = f32[3,6912]{1,0:T(4,128)} copy(f32[3,6912]{1,0:T(4,128)} %get-tuple-element.6) | data formatting | bytes 165888
  123.7 0.0 copy-done
  123.7 0.0 copy-start.1
  123.7 0.7 copy.14
  124.4 0.0 copy-done.1
  124.4 0.6 copy.15
Async XLA Ops:
  122.1 1.6 %copy-start = (f32[192,256]{1,0:T(8,128)S(1)}, f32[192,256]{1,0:T(8,128)}, u32[]{:S(2)}) copy-start(f32[192,256]{1,0:T(8,128)} %get-tuple-element.7) | copy-start | bytes 589828
  123.7 0.7 copy-start.1

commit v5 on v3

--- a/solution.py
+++ b/solution.py
@@ -14,7 +14,7 @@
 TILE = 8
 GROUP = 8
 LANES = 128
-UNROLL = 4
+UNROLL = 8
 
 center = 1.125
 half_width = 0.875
@@ -65,14 +65,21 @@
 
 
 def spread_low(rows, low_row, depth):
-    mask = lax.broadcasted_iota(i32, (depth, low_row.shape[1]), 0) == low_row
+    mask = low_mask(low_row, depth)
     tall = []
     for part in range(2):
         for row in rows:
             high = row.astype(bf16).astype(f32)
             piece = high if part == 0 else row - high
-            tall.append(jnp.where(mask, piece, 0.0).astype(bf16))
+            piece = jnp.broadcast_to(piece, (2 * TILE, row.shape[1])).astype(bf16)
+            piece = jnp.concatenate([piece] * (depth // (2 * TILE)), axis=0)
+            tall.append(jnp.where(mask, piece, jnp.zeros_like(piece)))
     return jnp.concatenate(tall, axis=0)
+
+
+def low_mask(low_row, depth):
+    numbers = lax.broadcasted_iota(i32, (depth, low_row.shape[1]), 0).astype(f32).astype(bf16)
+    return numbers == low_row.astype(f32).astype(bf16)
 
 
 def one_hot_rows(row, count):

time: 73.6 us -> 88.3 us (1.20); the launches traced: 73.4 us -> 87.1 us
  Pallas kernels: 69.9 us -> 83.6 us
    pallas_call x1, Pallas kernels: 69.9 us -> 83.6 us  [local(): pl.pallas_call(functools.partial(kernel, devices, subs), out_shape=(jax.S...]
where the time goes in v5:
time: 88.3 us; the launch traced here: 87.1 us
  Pallas kernels  83.6 us (95%)
  local copies, waits for them, and re-layouts  2.86 us (3%)
    pallas_call x1, Pallas kernels, local(): pl.pallas_call(functools.partial(kernel, devices, subs), out_shape=(jax.S...  83.6 us
    unnamed x7, local copies, waits for them, and re-layouts  2.86 us

profile of v5, /device:TPU:8, one launch (start us, length us, event | category | flops | bytes accessed | tf_op | source)
XLA Modules:
  0.0 87.1 jit_solution(73805722689474106)
XLA Ops:
  0.6 83.6 %migrate_and_smooth.1 = (f32[3,6912]{1,0:T(4,128)}, f32[192,256]{1,0:T(8,128)}, f32[2,256]{1,0:T(2,128)}) custom-call(f32[3,6912]{1,0:T(4,128)} %start_hbm.1, f32[192,256]{1,0:T(8,128)} %loads_hbm.1, f32[2,256]{1,0:T(2,128)} %coefs_ref.1, s32[64,256]{1,0:T(8,128)} %nodes_hbm.1, s32[3,256]{1,0:T(4,128)} %moves_ref.1, s32[2,192]{1,0:T(2,128)} %face_ref.1, ...), custom_call_target="tpu_custom_call" | custom-call | tf_op jit(solution)/shard_map/migrate_and_smooth/pallas_call | solution.py:514
  84.2 0.0 copy-start
  84.2 1.6 %copy.13 = f32[3,6912]{1,0:T(4,128)} copy(f32[3,6912]{1,0:T(4,128)} %get-tuple-element.6) | data formatting | bytes 165888
  85.8 0.0 copy-done
  85.8 0.0 copy-start.1
  85.8 0.7 copy.14
  86.5 0.0 copy-done.1
  86.5 0.6 copy.15
Async XLA Ops:
  84.2 1.6 %copy-start = (f32[192,256]{1,0:T(8,128)S(1)}, f32[192,256]{1,0:T(8,128)}, u32[]{:S(2)}) copy-start(f32[192,256]{1,0:T(8,128)} %get-tuple-element.7) | copy-start | bytes 589828
  85.8 0.7 copy-start.1
